TPU v7x, 128 devices: a whole 4x4x4 slice. The times are simulated.
128 devices in a mesh: dp: 16 (over y, x), expert: 8 (over z, core).
Axes of the slice: x: 4, y: 4, z: 4, core: 2. Of those that a mesh axis runs over, the one named last changes fastest.
Arguments:
- tokens: bfloat16 [16384, 1280], P(('dp', 'expert')), may hold values from -6 to 6
- cotangent: bfloat16 [16384, 1280], P(('dp', 'expert')), may hold values from -4 to 4
- gate_weights: float32 [16384, 2], P(('dp', 'expert')), may hold values from 0.1 to 1
- expert_ids: int32 [16384, 2], P(('dp', 'expert')), may hold values from 0 to 15, as said below
- segments: int32 [128, 128], P(('dp', 'expert')), may hold values from 0 to 3, never falling along the last dimension, each value on 1 to 64 neighbouring positions
- keep_counts: int32 [128, 4], P(('dp', 'expert')), may hold values from 1 to 64
- expand_weight: bfloat16 [16, 2560, 1280], P('expert', 'dp'), may hold values from -0.15625 to 0.15625
- reduce_weight: bfloat16 [16, 2560, 1280], P('expert', 'dp'), may hold values from -0.125 to 0.125
Outputs:
- output: bfloat16 [16384, 1280], P(('dp', 'expert'))
- tokens_grad: bfloat16 [16384, 1280], P(('dp', 'expert'))
- gating_grad: float32 [16384, 2], P(('dp', 'expert'))
- expand_grad: bfloat16 [16, 2560, 1280], P('expert', 'dp')
- reduce_grad: bfloat16 [16, 2560, 1280], P('expert', 'dp')
Inputs may be any that keep to these rules, and one draw needn't show every extreme that they name: `expert_ids`: the 128 tokens of one sequence name each expert exactly 16 times, and a token's 2 experts differ. `segments`: within a sequence the ids never fall, every image 0 to 3 appears, each holds 1 to 64 positions.
All inputs are finite; a program needn't handle non-finite values.
Results may differ from a plain program's by a relative error of at most 0.015.
Values may be sent and summed in bfloat16 or wider, within the bound.
A program may use at most 128 MiB of HBM per device.

v0:
```python
import jax
import jax.numpy as jnp
from jax import lax
from jax.sharding import PartitionSpec as P

epsilon = 1e-06
root_half = 0.7071067811865476
density_scale = 0.3989422804014327


def gelu_value(values):
    return 0.5 * values * (1.0 + jax.scipy.special.erf(values * root_half))


def gelu_slope(values):
    return (
        0.5 * (1.0 + jax.scipy.special.erf(values * root_half))
        + values * jnp.exp(-0.5 * values * values) * density_scale
    )


def project_up(rows, weight):
    return jnp.einsum("rld,lhd->rlh", rows, weight, preferred_element_type=jnp.float32)


def project_down(hidden, weight):
    return jnp.einsum("rlh,lhd->rld", hidden, weight, preferred_element_type=jnp.float32)


def outer_rows(left, right):
    return jnp.einsum("rlh,rld->lhd", left, right, preferred_element_type=jnp.float32)


def body(
    tokens, cotangent, gate_weights, expert_ids, segments, keep_counts, expand_weight, reduce_weight
):
    tok_count = tokens.shape[0]
    top_count = expert_ids.shape[1]
    width = tokens.shape[1]
    sources = lax.axis_size("expert")
    local = expand_weight.shape[0]
    total_experts = local * sources
    pick_count = top_count * tok_count
    capacity = pick_count // total_experts
    image_ids = segments[0]
    position = jnp.arange(tok_count, dtype=jnp.int32)
    earlier_img = jnp.sum((image_ids[None, :] < image_ids[:, None]).astype(jnp.int32), axis=1)
    image_match = (
        image_ids[:, None] == jnp.arange(keep_counts.shape[1], dtype=jnp.int32)[None, :]
    ).astype(jnp.int32)
    keep_token = jnp.sum(image_match * keep_counts, axis=1)
    alive = (position - earlier_img < keep_token).astype(jnp.float32)
    tokens_wide = tokens.astype(jnp.float32)
    mean_rows = jnp.mean(tokens_wide, axis=1, keepdims=True)
    centred = tokens_wide - mean_rows
    inv_scale = lax.rsqrt(jnp.mean(centred * centred, axis=1, keepdims=True) + epsilon)
    normed = centred * inv_scale
    normed_low = normed.astype(jnp.bfloat16)
    choice_list = expert_ids.reshape(-1)
    matches = (choice_list[:, None] == jnp.arange(total_experts, dtype=jnp.int32)[None, :]).astype(
        jnp.int32
    )
    before = jnp.cumsum(matches, axis=0) - matches
    slot_list = jnp.sum(before * matches, axis=1)
    target = choice_list * capacity + slot_list
    order = (
        jnp.zeros((pick_count,), jnp.int32).at[target].set(jnp.arange(pick_count, dtype=jnp.int32))
    )
    source = order // top_count
    alive_pick = jnp.repeat(alive, top_count)
    weight_pick = gate_weights.reshape(-1) * alive_pick
    sent_rows = jnp.where(
        alive_pick[order][:, None] > 0, normed_low[source], jnp.zeros((), jnp.bfloat16)
    )
    cot_wide = cotangent.astype(jnp.float32)
    sent_grads = (cot_wide[source] * weight_pick[order][:, None]).astype(jnp.bfloat16)

    def to_slots(flat):
        return (
            flat.reshape(sources, local, capacity, width)
            .transpose(0, 2, 1, 3)
            .reshape(sources * capacity, local, width)
        )

    def from_slots(rows):
        return (
            rows.reshape(sources, capacity, local, width)
            .transpose(0, 2, 1, 3)
            .reshape(pick_count, width)
        )

    arrived = to_slots(lax.all_to_all(sent_rows, "expert", split_axis=0, concat_axis=0, tiled=True))
    arrived_grads = to_slots(
        lax.all_to_all(sent_grads, "expert", split_axis=0, concat_axis=0, tiled=True)
    )
    slot_rows = arrived.shape[0]
    all_rows = lax.all_gather(arrived, "dp", axis=0, tiled=True)
    pre = project_up(all_rows, expand_weight)
    hidden = gelu_value(pre).astype(jnp.bfloat16)
    results = lax.psum_scatter(
        project_down(hidden, reduce_weight).astype(jnp.bfloat16),
        "dp",
        scatter_dimension=0,
        tiled=True,
    )
    all_grads = lax.all_gather(arrived_grads, "dp", axis=0, tiled=True)
    back_hidden = project_up(all_grads, reduce_weight)
    dpre = (back_hidden * gelu_slope(pre)).astype(jnp.bfloat16)
    input_rows = lax.psum_scatter(
        project_down(dpre, expand_weight).astype(jnp.bfloat16),
        "dp",
        scatter_dimension=0,
        tiled=True,
    )

    def add_block(block, totals):
        offset = block * slot_rows
        hidden_block = lax.dynamic_slice_in_dim(hidden, offset, slot_rows, 0)
        dpre_block = lax.dynamic_slice_in_dim(dpre, offset, slot_rows, 0)
        grad_block = lax.dynamic_slice_in_dim(all_grads, offset, slot_rows, 0)
        row_block = lax.dynamic_slice_in_dim(all_rows, offset, slot_rows, 0)
        second_piece = lax.optimization_barrier(
            outer_rows(hidden_block, grad_block).astype(jnp.bfloat16)
        ).astype(jnp.float32)
        first_piece = lax.optimization_barrier(
            outer_rows(dpre_block, row_block).astype(jnp.bfloat16)
        ).astype(jnp.float32)
        return (totals[0] + first_piece, totals[1] + second_piece)

    empty = jnp.zeros(expand_weight.shape, jnp.float32)
    first_total, second_total = lax.fori_loop(
        0, all_rows.shape[0] // slot_rows, add_block, (empty, empty)
    )
    expand_grad = first_total.astype(jnp.bfloat16)
    reduce_grad = second_total.astype(jnp.bfloat16)
    returned = lax.all_to_all(
        from_slots(results), "expert", split_axis=0, concat_axis=0, tiled=True
    )
    result_pick = returned[target].astype(jnp.float32).reshape(tok_count, top_count, -1)
    output = (
        tokens_wide + jnp.sum(result_pick * weight_pick.reshape(tok_count, top_count, 1), axis=1)
    ).astype(jnp.bfloat16)
    gating_grad = alive_pick.reshape(tok_count, top_count) * jnp.sum(
        cot_wide[:, None, :] * result_pick, axis=2
    )
    returned_grads = lax.all_to_all(
        from_slots(input_rows), "expert", split_axis=0, concat_axis=0, tiled=True
    )
    input_pick = returned_grads[target].astype(jnp.float32).reshape(tok_count, top_count, -1)
    grad_norm = jnp.sum(input_pick * alive_pick.reshape(tok_count, top_count, 1), axis=1)
    tokens_grad = cot_wide + inv_scale * (
        grad_norm
        - jnp.mean(grad_norm, axis=1, keepdims=True)
        - normed * jnp.mean(grad_norm * normed, axis=1, keepdims=True)
    )
    return (output, tokens_grad.astype(jnp.bfloat16), gating_grad, expand_grad, reduce_grad)


def solution(mesh):
    in_specs = (
        P(("dp", "expert"), None),
        P(("dp", "expert"), None),
        P(("dp", "expert"), None),
        P(("dp", "expert"), None),
        P(("dp", "expert"), None),
        P(("dp", "expert"), None),
        P("expert", "dp", None),
        P("expert", "dp", None),
    )
    out_specs = (
        P(("dp", "expert"), None),
        P(("dp", "expert"), None),
        P(("dp", "expert"), None),
        P("expert", "dp", None),
        P("expert", "dp", None),
    )
    return jax.shard_map(body, mesh=mesh, in_specs=in_specs, out_specs=out_specs, check_vma=False)
```

profile of v0, /device:TPU:1, one launch (start us, length us, event | category | flops | bytes accessed | tf_op | source)
XLA Modules:
  0.0 434.9 jit_solution(15564184737724795476)
XLA Ops:
  16.0 1.9 gather_fusion
  19.6 17.6 %all_to_all.36 = bf16[8,32,1280]{2,1,0:T(8,128)(2,1)S(1)} all-to-all(bf16[8,32,1280]{2,1,0:T(8,128)(2,1)S(1)} %broadcast_select_fusion), channel_id=1, replica_groups=mesh['dp'=16,'expert'=8] {'expert'}, dimensions={0} | all-to-all | bytes 1310720 | tf_op jit(solution)/shard_map/all_to_all | solution.py:92
  38.4 1.9 gather_fusion.4
  41.9 14.2 %all_to_all.37 = bf16[8,32,1280]{2,1,0:T(8,128)(2,1)S(1)} all-to-all(bf16[8,32,1280]{2,1,0:T(8,128)(2,1)S(1)} %multiply_convert_fusion.1), channel_id=1, replica_groups=mesh['dp'=16,'expert'=8] {'expert'}, dimensions={0} | all-to-all | bytes 1310720 | tf_op jit(solution)/shard_map/all_to_all | solution.py:94
  57.1 61.1 %all-gather.3.cloned.1.call-done = bf16[2048,2,1280]{2,0,1:T(8,128)(2,1)} async-done(((bf16[128,2,1280]{2,0,1:T(8,128)(2,1)}), bf16[2048,2,1280]{2,0,1:T(8,128)(2,1)}) %all-gather.3.cloned.1.call-update) | async-done | bytes 10485776 | tf_op jit(solution)/shard_map/all_gather | solution.py:97
  118.2 9.1 %multiply_convert_fusion = (bf16[2048,2,160]{0,2,1:T(8,128)(2,1)S(1)}, f32[2048,2,160]{0,2,1:T(8,128)}) fusion(bf16[2048,2,1280]{2,0,1:T(8,128)(2,1)} %all-gather.3.cloned.1.call-done, bf16[2,160,1280]{2,1,0:T(8,128)(2,1)S(1)} %copy-done), kind=kOutput, calls=%fused_computation.30 | convolution fusion | flops 1680998400 | bytes 15237120 | tf_op jit(solution)/shard_map/rld,lhd->rlh/dot_general | solution.py:23
  127.3 73.6 %all-gather.5.cloned.1.call-done = bf16[2048,2,1280]{2,0,1:T(8,128)(2,1)} async-done(((bf16[128,2,1280]{2,0,1:T(8,128)(2,1)}), bf16[2048,2,1280]{2,0,1:T(8,128)(2,1)}) %all-gather.5.cloned.1.call-update) | async-done | bytes 10485776 | tf_op jit(solution)/shard_map/all_gather | solution.py:106
  200.9 8.6 %fusion.9 = bf16[2048,2,160]{0,2,1:T(8,128)(2,1)S(1)} fusion(bf16[2048,2,1280]{2,0,1:T(8,128)(2,1)} %all-gather.5.cloned.1.call-done, bf16[2,160,1280]{2,1,0:T(8,128)(2,1)} %param.17, f32[2048,2,160]{0,2,1:T(8,128)} %get-tuple-element.189), kind=kOutput, calls=%fused_computation.25 | convolution fusion | flops 1684275200 | bytes 15237120 | tf_op jit(solution)/shard_map/rld,lhd->rlh/dot_general | solution.py:23
  210.6 5.6 %fusion.7 = bf16[2048,2,1280]{2,0,1:T(8,128)(2,1)} fusion(bf16[2048,2,160]{0,2,1:T(8,128)(2,1)S(1)} %fusion.9, bf16[2,160,1280]{2,1,0:T(8,128)(2,1)S(1)} %copy-done), kind=kOutput, calls=%fused_computation.20 | convolution fusion | flops 1682964480 | bytes 12615680 | tf_op jit(solution)/shard_map/rlh,lhd->rld/dot_general | solution.py:27
  217.3 5.7 %fusion.6 = bf16[2048,2,1280]{2,0,1:T(8,128)(2,1)} fusion(bf16[2048,2,160]{0,2,1:T(8,128)(2,1)S(1)} %get-tuple-element.244, bf16[2,160,1280]{2,1,0:T(8,128)(2,1)S(1)} %copy-done.10), kind=kOutput, calls=%fused_computation.19 | convolution fusion | flops 1682964480 | bytes 12615680 | tf_op jit(solution)/shard_map/rlh,lhd->rld/dot_general | solution.py:27
  223.1 81.8 %reduce-scatter.5.cloned.1.call-done = bf16[128,2,1280]{2,0,1:T(8,128)(2,1)} async-done(((bf16[2048,2,1280]{2,0,1:T(8,128)(2,1)}), bf16[128,2,1280]{2,0,1:T(8,128)(2,1)}) %reduce-scatter.5.cloned.1.call-update) | async-done | bytes 655376 | tf_op jit(solution)/shard_map/reduce_scatter | solution.py:109
  304.9 2.0 copy.47
  306.9 5.9 %all-to-all-start.3 = ((bf16[8,32,1280]{2,1,0:T(8,128)(2,1)}), bf16[8,32,1280]{2,1,0:T(8,128)(2,1)}, u32[]{:S(2)}, u32[]{:S(2)}) async-start(bf16[8,32,1280]{2,1,0:T(8,128)(2,1)} %bitcast.23), calls=%async_computation.5 | async-start | bytes 1310720 | tf_op jit(solution)/shard_map/all_to_all | solution.py:146
  312.8 86.8 %while.16 = (s32[]{:T(128)}, f32[2,160,1280]{2,1,0:T(8,128)}, f32[2,160,1280]{2,1,0:T(8,128)S(1)}, bf16[2048,2,160]{0,2,1:T(8,128)(2,1)}, bf16[2048,2,1280]{2,0,...) while((s32[]{:T(128)}, f32[2,160,1280]{2,1,0:T(8,128)}, ...), condition=%wide.region_17.18_spmd.clone, body=%wide.region_16.17_spmd.clone.sunk | while | flops 212992000 | bytes 24414436 | solution.py:131
  318.2 1.6 convolution_convert_fusion.6
  323.6 1.6 convolution_convert_fusion.6
  329.1 1.6 convolution_convert_fusion.6
  334.6 1.6 convolution_convert_fusion.6
  340.0 1.6 convolution_convert_fusion.6
  350.9 1.6 convolution_convert_fusion.6
  361.8 1.6 convolution_convert_fusion.6
  367.2 1.6 convolution_convert_fusion.6
  388.8 1.6 convolution_convert_fusion.6
  394.2 1.6 convolution_convert_fusion.6
  402.3 2.0 copy.42
  404.3 4.8 %all-to-all-start.1 = ((bf16[8,32,1280]{2,1,0:T(8,128)(2,1)}), bf16[8,32,1280]{2,1,0:T(8,128)(2,1)S(1)}, u32[]{:S(2)}, u32[]{:S(2)}) async-start(bf16[8,32,1280]{2,1,0:T(8,128)(2,1)} %bitcast.13), calls=%async_computation.2 | async-start | bytes 1310720 | tf_op jit(solution)/shard_map/all_to_all | solution.py:136
  409.1 2.9 gather_fusion.5
  412.4 1.7 reshape.174
  414.2 3.0 multiply_reduce_fusion.2
  417.6 2.5 all-to-all-done.1
  421.3 1.7 reshape.173
  423.0 3.5 multiply_reduce_fusion
  (189 shorter events, 93.0 us)
Async XLA Ops:
  7.2 111.0 %copy-start = (bf16[2,160,1280]{2,1,0:T(8,128)(2,1)S(1)}, bf16[2,160,1280]{2,1,0:T(8,128)(2,1)}, u32[]{:S(2)}) copy-start(bf16[2,160,1280]{2,1,0:T(8,128)(2,1)} %param.16) | copy-start | bytes 2457604
  7.2 10.8 %copy-start.5 = (bf16[128,1280]{1,0:T(8,128)(2,1)S(1)}, bf16[128,1280]{1,0:T(8,128)(2,1)}, u32[]{:S(2)}) copy-start(bf16[128,1280]{1,0:T(8,128)(2,1)} %param.10) | copy-start | bytes 983044
  7.2 111.0 %all-gather.3.cloned.1.call-start = ((), (), s32[]{:S(2)}) async-start(), calls=%async_computation.6 | async-start | bytes 11141120 | tf_op jit(solution)/shard_map/all_gather | solution.py:97
  19.6 18.5 %copy-start.11 = (f32[128,2]{0,1:T(2,128)S(1)}, f32[128,2]{0,1:T(2,128)}, u32[]{:S(2)}) copy-start(f32[128,2]{0,1:T(2,128)} %param.12) | copy-start | bytes 3076
  37.2 3.3 copy-start.8
  38.1 162.8 %all-gather.5.cloned.1.call-start = ((), (), s32[]{:S(2)}) async-start(), calls=%async_computation.8 | async-start | bytes 11141120 | tf_op jit(solution)/shard_map/all_gather | solution.py:106
  57.0 247.9 %reduce-scatter.5.cloned.1.call-start = ((), (), s32[]{:S(2)}) async-start(), calls=%async_computation.9 | async-start | bytes 11141120 | tf_op jit(solution)/shard_map/reduce_scatter | solution.py:109
  127.3 89.1 %copy-start.6 = (bf16[2048,2,160]{0,2,1:T(8,128)(2,1)}, bf16[2048,2,160]{0,2,1:T(8,128)(2,1)S(1)}, u32[]{:S(2)}) copy-start(bf16[2048,2,160]{0,2,1:T(8,128)(2,1)S(1)} %get-tuple-element.244) | copy-start | bytes 3932164
  216.2 186.2 %reduce-scatter.3.cloned.1.call-start = ((), (), s32[]{:S(2)}) async-start(), calls=%async_computation.7 | async-start | bytes 11141120 | tf_op jit(solution)/shard_map/reduce_scatter | solution.py:100
  306.9 97.5 %all-to-all-start.3 = ((bf16[8,32,1280]{2,1,0:T(8,128)(2,1)}), bf16[8,32,1280]{2,1,0:T(8,128)(2,1)}, u32[]{:S(2)}, u32[]{:S(2)}) async-start(bf16[8,32,1280]{2,1,0:T(8,128)(2,1)} %bitcast.23), calls=%async_computation.5 | async-start | bytes 1310720 | tf_op jit(solution)/shard_map/all_to_all | solution.py:146
  312.8 3.1 copy-start.2
  317.0 1.2 copy-start.3
  318.2 3.1 copy-start.2
  322.5 1.2 copy-start.3
  323.6 3.2 copy-start.2
  329.1 3.2 copy-start.2
  334.6 3.2 copy-start.2
  340.0 3.2 copy-start.2
  345.5 3.1 copy-start.2
  350.9 3.1 copy-start.2
  356.3 3.1 copy-start.2
  361.8 3.1 copy-start.2
  367.2 3.1 copy-start.2
  372.6 3.1 copy-start.2
  378.0 3.1 copy-start.2
  383.4 3.1 copy-start.2
  388.8 3.2 copy-start.2
  394.2 3.2 copy-start.2
  399.6 1.7 copy-start.4
  404.3 15.7 %all-to-all-start.1 = ((bf16[8,32,1280]{2,1,0:T(8,128)(2,1)}), bf16[8,32,1280]{2,1,0:T(8,128)(2,1)S(1)}, u32[]{:S(2)}, u32[]{:S(2)}) async-start(bf16[8,32,1280]{2,1,0:T(8,128)(2,1)} %bitcast.13), calls=%async_computation.2 | async-start | bytes 1310720 | tf_op jit(solution)/shard_map/all_to_all | solution.py:136
  423.0 4.2 copy-start.9
  423.0 5.4 %copy-start.1 = (bf16[2,160,1280]{2,1,0:T(8,128)(2,1)S(1)}, bf16[2,160,1280]{2,1,0:T(8,128)(2,1)}, u32[]{:S(2)}) copy-start(bf16[2,160,1280]{2,1,0:T(8,128)(2,1)} %param.16) | copy-start | bytes 2457604
  (16 other events, 18.8 us)
Sparse Core Ops, SparseCore 0:
  38.2 79.9 all-gather.2
  120.9 79.9 all-gather.4
  216.3 88.5 reduce-scatter.4
  308.2 88.6 reduce-scatter.2
where the time goes:
time: 436 us; the launch traced here: 435 us
  waiting for transfers between devices  219 us (50%)
  matrix products  79 us (18%)
  local copies, waits for them, and re-layouts  45.8 us (11%)
  other arithmetic  33.5 us (8%)
  blocking collectives  31.8 us (7%)
  between operations  14 us (3%)
  starting transfers between devices  11.1 us (3%)
    reduce_scatter x1, waiting for transfers between devices, body(): lax.psum_scatter(project_down(dpre, expand_weight).astype(jnp.bfloat16),...  81.8 us
    all_gather x1, waiting for transfers between devices, body(): all_grads = lax.all_gather(arrived_grads, 'dp', axis=0, tiled=True)  73.6 us
    all_gather x1, waiting for transfers between devices, body(): all_rows = lax.all_gather(arrived, 'dp', axis=0, tiled=True)  61.1 us
    dot_general x32, matrix products, outer_rows(): jnp.einsum('rlh,rld->lhd', left, right, preferred_element_type=jnp.float32)  50.1 us
    while x64, local copies, waits for them, and re-layouts  19 us
    dot_general x2, matrix products, project_up(): jnp.einsum('rld,lhd->rlh', rows, weight, preferred_element_type=jnp.float32)  17.7 us
    all_to_all x1, blocking collectives, body(): lax.all_to_all(sent_rows, 'expert', split_axis=0, concat_axis=0, tiled=True)  17.6 us
    add x16, other arithmetic, add_block(): return (totals[0] + first_piece, totals[1] + second_piece)  17.2 us
  transfers between devices with their start and end apart: 6, of which 4 were waited for; matrix products, arithmetic and copies ran while one was open for 23% of the time, Pallas kernels for 0%

commit v1 on v0

--- a/solution.py
+++ b/solution.py
@@ -103,7 +103,9 @@
         scatter_dimension=0,
         tiled=True,
     )
-    all_grads = lax.all_gather(arrived_grads, "dp", axis=0, tiled=True)
+    all_grads = jnp.concatenate(
+        lax.all_to_all(jnp.stack([arrived_grads] * lax.axis_size("dp")), "dp", 0, 0), axis=0
+    )
     back_hidden = project_up(all_grads, reduce_weight)
     dpre = (back_hidden * gelu_slope(pre)).astype(jnp.bfloat16)
     input_rows = lax.psum_scatter(

time: 436 us -> 499 us (1.14)
  blocking collectives: 31.8 us -> 198 us
  waiting for transfers between devices: 219 us -> 81.3 us
  other arithmetic: 33.5 us -> 75.5 us
  local copies, waits for them, and re-layouts: 45.8 us -> 39.1 us
    all_to_all x0 -> x1, blocking collectives: none -> 166 us  [body(): lax.all_to_all(jnp.stack([arrived_grads] * lax.axis_size('dp')), 'dp', 0, 0)]
    all_gather x1 -> x0, waiting for transfers between devices: 73.6 us -> none  [body(): all_grads = lax.all_gather(arrived_grads, 'dp', axis=0, tiled=True)]
    all_gather x1, waiting for transfers between devices: 61.1 us -> 0.01 us  [body(): all_rows = lax.all_gather(arrived, 'dp', axis=0, tiled=True)]
    add x16, other arithmetic: 17.2 us -> 58.2 us  [add_block(): return (totals[0] + first_piece, totals[1] + second_piece)]
    while x64 -> x0, local copies, waits for them, and re-layouts: 19 us -> none
    all_to_all x0 -> x1, local copies, waits for them, and re-layouts: none -> 8.94 us  [body(): lax.all_to_all(jnp.stack([arrived_grads] * lax.axis_size('dp')), 'dp', 0, 0)]
    another operation x1 -> x2, local copies, waits for them, and re-layouts: 0.01 us -> 5.02 us  [the longest x1 5.02 us: body(): jnp.stack([arrived_grads] * lax.axis_size('dp'))]
  transfers between devices with their start and end apart: 6 -> 5, of which waited for: 4 -> 2; matrix products, arithmetic and copies ran while one was open for 23% -> 29% of each run, Pallas kernels for 0% -> 0%
where the time goes in v1:
time: 499 us; the launch traced here: 497 us
  blocking collectives  198 us (40%)
  waiting for transfers between devices  81.3 us (16%)
  matrix products  78.2 us (16%)
  other arithmetic  75.5 us (15%)
  local copies, waits for them, and re-layouts  39.1 us (8%)
  between operations  14 us (3%)
  starting transfers between devices  10.7 us (2%)
    all_to_all x1, blocking collectives, body(): lax.all_to_all(jnp.stack([arrived_grads] * lax.axis_size('dp')), 'dp', 0, 0)  166 us
    reduce_scatter x1, waiting for transfers between devices, body(): lax.psum_scatter(project_down(dpre, expand_weight).astype(jnp.bfloat16),...  78.8 us
    add x16, other arithmetic, add_block(): return (totals[0] + first_piece, totals[1] + second_piece)  58.2 us
    dot_general x32, matrix products, outer_rows(): jnp.einsum('rlh,rld->lhd', left, right, preferred_element_type=jnp.float32)  48.7 us
    all_to_all x1, blocking collectives, body(): lax.all_to_all(sent_rows, 'expert', split_axis=0, concat_axis=0, tiled=True)  17.7 us
    dot_general x2, matrix products, project_up(): jnp.einsum('rld,lhd->rlh', rows, weight, preferred_element_type=jnp.float32)  15.6 us
    all_to_all x1, blocking collectives, body(): lax.all_to_all(sent_grads, 'expert', split_axis=0, concat_axis=0, tiled=T...  14.2 us
    dot_general x2, matrix products, project_down(): jnp.einsum('rlh,lhd->rld', hidden, weight, preferred_element_type=jnp.flo...  13.9 us
  transfers between devices with their start and end apart: 5, of which 2 were waited for; matrix products, arithmetic and copies ran while one was open for 29% of the time, Pallas kernels for 0%

profile of v1, /device:TPU:1, one launch (start us, length us, event | category | flops | bytes accessed | tf_op | source)
XLA Modules:
  0.0 497.2 jit_solution(322649769619000075)
XLA Ops:
  20.5 17.7 %all_to_all.41 = bf16[8,32,1280]{2,1,0:T(8,128)(2,1)S(1)} all-to-all(bf16[8,32,1280]{2,1,0:T(8,128)(2,1)S(1)} %broadcast_select_fusion), channel_id=1, replica_groups=mesh['dp'=16,'expert'=8] {'expert'}, dimensions={0} | all-to-all | bytes 1310720 | tf_op jit(solution)/shard_map/all_to_all | solution.py:92
  42.9 14.2 %all_to_all.42 = bf16[8,32,1280]{2,1,0:T(8,128)(2,1)S(1)} all-to-all(bf16[8,32,1280]{2,1,0:T(8,128)(2,1)S(1)} %multiply_convert_fusion.1), channel_id=1, replica_groups=mesh['dp'=16,'expert'=8] {'expert'}, dimensions={0} | all-to-all | bytes 1310720 | tf_op jit(solution)/shard_map/all_to_all | solution.py:94
  57.2 5.0 %stack.3 = bf16[16,128,2,1280]{3,1,2,0:T(8,128)(2,1)} broadcast(bf16[128,2,1280]{2,0,1:T(8,128)(2,1)S(1)} %bitcast.72), dimensions={1,2,3} | broadcast | bytes 11141120 | tf_op jit(solution)/shard_map/stack | solution.py:107
  62.2 166.1 %all_to_all.43 = bf16[16,128,2,1280]{3,1,2,0:T(8,128)(2,1)} all-to-all(bf16[16,128,2,1280]{3,1,2,0:T(8,128)(2,1)} %stack.3), channel_id=1, replica_groups=mesh['dp'=16,'expert'=8] {'dp'}, dimensions={0} | all-to-all | bytes 20971520 | tf_op jit(solution)/shard_map/all_to_all | solution.py:107
  228.4 8.9 %copy.49 = bf16[16,128,2,1280]{3,1,0,2:T(8,128)(2,1)} copy(bf16[16,128,2,1280]{3,1,2,0:T(8,128)(2,1)} %all_to_all.43) | data formatting | bytes 20971520 | tf_op jit(solution)/shard_map/all_to_all | solution.py:107
  237.3 6.3 %multiply_convert_fusion = (bf16[2048,2,160]{0,2,1:T(8,128)(2,1)S(1)}, f32[2048,2,160]{0,2,1:T(8,128)S(1)}) fusion(bf16[2048,2,1280]{2,0,1:T(8,128)(2,1)} %all-gather.2.cloned.1.call-done, bf16[2,160,1280]{2,1,0:T(8,128)(2,1)S(1)} %copy-done), kind=kOutput, calls=%fused_computation.30 | convolution fusion | flops 1680998400 | bytes 15237120 | tf_op jit(solution)/shard_map/rld,lhd->rlh/dot_general | solution.py:23
  243.6 9.3 %fusion.9 = bf16[2048,2,160]{0,2,1:T(8,128)(2,1)} fusion(bf16[2048,2,1280]{2,0,1:T(8,128)(2,1)} %bitcast.65, bf16[2,160,1280]{2,1,0:T(8,128)(2,1)} %param.17, f32[2048,2,160]{0,2,1:T(8,128)S(1)} %get-tuple-element.189), kind=kOutput, calls=%fused_computation.25 | convolution fusion | flops 1684275200 | bytes 15237120 | tf_op jit(solution)/shard_map/rld,lhd->rlh/dot_general | solution.py:23
  253.0 8.1 %fusion.7 = bf16[2048,2,1280]{2,0,1:T(8,128)(2,1)} fusion(bf16[2048,2,160]{0,2,1:T(8,128)(2,1)} %fusion.9, bf16[2,160,1280]{2,1,0:T(8,128)(2,1)S(1)} %copy-done), kind=kOutput, calls=%fused_computation.20 | convolution fusion | flops 1682964480 | bytes 12615680 | tf_op jit(solution)/shard_map/rlh,lhd->rld/dot_general | solution.py:27
  262.3 5.8 %fusion.6 = bf16[2048,2,1280]{2,0,1:T(8,128)(2,1)} fusion(bf16[2048,2,160]{0,2,1:T(8,128)(2,1)S(1)} %get-tuple-element.244, bf16[2,160,1280]{2,1,0:T(8,128)(2,1)S(1)} %copy-done.6), kind=kOutput, calls=%fused_computation.19 | convolution fusion | flops 1682964480 | bytes 12615680 | tf_op jit(solution)/shard_map/rlh,lhd->rld/dot_general | solution.py:27
  268.2 78.8 %reduce-scatter.5.cloned.1.call-done = bf16[128,2,1280]{2,0,1:T(8,128)(2,1)} async-done(((bf16[2048,2,1280]{2,0,1:T(8,128)(2,1)}), bf16[128,2,1280]{2,0,1:T(8,128)(2,1)}) %reduce-scatter.5.cloned.1.call-update) | async-done | bytes 655376 | tf_op jit(solution)/shard_map/reduce_scatter | solution.py:111
  348.9 6.0 %all-to-all-start.4 = ((bf16[8,32,1280]{2,1,0:T(8,128)(2,1)}), bf16[8,32,1280]{2,1,0:T(8,128)(2,1)}, u32[]{:S(2)}, u32[]{:S(2)}) async-start(bf16[8,32,1280]{2,1,0:T(8,128)(2,1)} %bitcast.24), calls=%async_computation.6 | async-start | bytes 1310720 | tf_op jit(solution)/shard_map/all_to_all | solution.py:148
  354.9 107.2 %while.16 = (s32[]{:T(128)}, f32[2,160,1280]{2,1,0:T(8,128)S(1)}, f32[2,160,1280]{2,1,0:T(8,128)}, bf16[2048,2,160]{0,2,1:T(8,128)(2,1)}, bf16[2048,2,1280]{2,0,...) while((s32[]{:T(128)}, f32[2,160,1280]{2,1,0:T(8,128)S(1)}, ...), condition=%wide.region_17.18_spmd.clone, body=%wide.region_16.17_spmd.clone.sunk | while | flops 212992000 | bytes 11307181 | solution.py:133
  363.3 3.7 select_add_fusion.3
  370.0 3.7 select_add_fusion.3
  376.9 3.7 select_add_fusion.3
  383.7 3.8 select_add_fusion.3
  390.6 3.7 select_add_fusion.3
  397.5 3.8 select_add_fusion.3
  404.3 3.7 select_add_fusion.3
  411.1 3.7 select_add_fusion.3
  417.8 3.7 select_add_fusion.3
  424.8 3.7 select_add_fusion.3
  431.5 3.7 select_add_fusion.3
  438.3 3.7 select_add_fusion.3
  445.0 3.7 select_add_fusion.3
  451.7 3.7 select_add_fusion.3
  458.4 3.7 select_add_fusion.3
  466.9 4.6 all-to-all-start.1
  471.5 2.9 gather_fusion.5
  476.4 3.0 multiply_reduce_fusion.2
  479.9 2.5 all-to-all-done.1
  485.3 3.5 multiply_reduce_fusion
  (121 shorter events, 84.2 us)
Async XLA Ops:
  7.2 230.2 %copy-start = (bf16[2,160,1280]{2,1,0:T(8,128)(2,1)S(1)}, bf16[2,160,1280]{2,1,0:T(8,128)(2,1)}, u32[]{:S(2)}) copy-start(bf16[2,160,1280]{2,1,0:T(8,128)(2,1)} %param.16) | copy-start | bytes 2457604
  7.2 230.2 %all-gather.2.cloned.1.call-start = ((), (), s32[]{:S(2)}) async-start(), calls=%async_computation.7 | async-start | bytes 11141120 | tf_op jit(solution)/shard_map/all_gather | solution.py:97
  20.5 18.7 %copy-start.5 = (bf16[128,1280]{1,0:T(8,128)(2,1)S(1)}, bf16[128,1280]{1,0:T(8,128)(2,1)}, u32[]{:S(2)}) copy-start(bf16[128,1280]{1,0:T(8,128)(2,1)} %param.11) | copy-start | bytes 983044
  39.1 307.8 %reduce-scatter.5.cloned.1.call-start = ((), (), s32[]{:S(2)}) async-start(), calls=%async_computation.9 | async-start | bytes 11141120 | tf_op jit(solution)/shard_map/reduce_scatter | solution.py:111
  39.2 1.2 copy-start.7
  243.6 17.6 %copy-start.4 = (bf16[2048,2,160]{0,2,1:T(8,128)(2,1)}, bf16[2048,2,160]{0,2,1:T(8,128)(2,1)S(1)}, u32[]{:S(2)}) copy-start(bf16[2048,2,160]{0,2,1:T(8,128)(2,1)S(1)} %get-tuple-element.244) | copy-start | bytes 3932164
  261.1 1.1 copy-start.6
  261.1 203.7 %reduce-scatter.3.cloned.1.call-start = ((), (), s32[]{:S(2)}) async-start(), calls=%async_computation.8 | async-start | bytes 11141120 | tf_op jit(solution)/shard_map/reduce_scatter | solution.py:100
  348.9 117.9 %all-to-all-start.4 = ((bf16[8,32,1280]{2,1,0:T(8,128)(2,1)}), bf16[8,32,1280]{2,1,0:T(8,128)(2,1)}, u32[]{:S(2)}, u32[]{:S(2)}) async-start(bf16[8,32,1280]{2,1,0:T(8,128)(2,1)} %bitcast.24), calls=%async_computation.6 | async-start | bytes 1310720 | tf_op jit(solution)/shard_map/all_to_all | solution.py:148
  462.1 1.7 copy-start.2
  466.9 15.5 %all-to-all-start.1 = ((bf16[8,32,1280]{2,1,0:T(8,128)(2,1)}), bf16[8,32,1280]{2,1,0:T(8,128)(2,1)S(1)}, u32[]{:S(2)}, u32[]{:S(2)}) async-start(bf16[8,32,1280]{2,1,0:T(8,128)(2,1)} %bitcast.13), calls=%async_computation.2 | async-start | bytes 1310720 | tf_op jit(solution)/shard_map/all_to_all | solution.py:138
  476.1 3.5 copy-start.3
  485.3 5.4 %copy-start.1 = (bf16[2,160,1280]{2,1,0:T(8,128)(2,1)S(1)}, bf16[2,160,1280]{2,1,0:T(8,128)(2,1)}, u32[]{:S(2)}) copy-start(bf16[2,160,1280]{2,1,0:T(8,128)(2,1)} %param.16) | copy-start | bytes 2457604
Sparse Core Ops, SparseCore 0:
  39.3 183.9 all-gather.1
  261.3 85.6 reduce-scatter.4
  350.4 89.0 reduce-scatter.2
